TPU v7x, 32 devices: a whole 2x2x4 slice. The times are simulated.
32 devices in a mesh: outer: 4 (over y, x), inner: 8 (over z, core).
Axes of the slice: x: 2, y: 2, z: 4, core: 2. Of those that a mesh axis runs over, the one named last changes fastest.
Arguments:
- points: float32 [3584, 256], P(('outer', 'inner')), may hold values from -36 to 36
- vectors: float32 [3584, 128], P(('outer', 'inner')), may hold values from -6 to 6
- lengthscales: float32 [256], replicated, may hold values from 8 to 32
- outputscale: float32 [1], replicated, may hold values from 0.03 to 0.12
- noise: float32 [1], replicated, may hold values from 0.3 to 3
Outputs:
- product: float32 [3584, 128], P(('outer', 'inner'))
All inputs are finite; a program needn't handle non-finite values.
Results may differ from a plain program's by a relative error of at most 0.00024.
Values sent between devices are 32-bit elements; how exact they have to be, the bound alone decides.
No kernel may reach another device: no remote copies, remote signals or barrier semaphores. Data moves between devices by JAX's collectives and lax.ppermute only.
A program may use at most 128 MiB of HBM per device.

v0:
```python
import jax
import jax.numpy as jnp
from jax import lax
from jax.sharding import PartitionSpec as P


def matern(dist2, amplitude):
    scaled_r = jnp.sqrt(5.0) * jnp.sqrt(jnp.maximum(dist2, 0.0))
    return amplitude * (1.0 + scaled_r + scaled_r * scaled_r / 3.0) * jnp.exp(-scaled_r)


def row_norms(rows):
    return jnp.sum(rows * rows, axis=1)


def kernel_tile(rows, norms_here, cols, col_norms, amplitude):
    inner_prod = jnp.dot(
        rows, cols.T, precision=lax.Precision.HIGHEST, preferred_element_type=jnp.float32
    )
    dist2 = norms_here[:, None] + col_norms[None, :] - 2.0 * inner_prod
    return matern(dist2, amplitude)


def apply_tile(tile, values):
    return jnp.dot(
        tile, values, precision=lax.Precision.HIGHEST, preferred_element_type=jnp.float32
    )


def per_device(points, vectors, lengthscales, outputscale, noise):
    amplitude = outputscale[0]
    scaled = points / lengthscales[None, :]
    sqnorm = row_norms(scaled)
    piece_rows = lax.all_gather(scaled, ("outer", "inner"), axis=0, tiled=True)
    piece_values = lax.all_gather(vectors, ("outer", "inner"), axis=0, tiled=True)
    tile = kernel_tile(scaled, sqnorm, piece_rows, row_norms(piece_rows), amplitude)
    total = apply_tile(tile, piece_values)
    return total + noise[0] * vectors


def solution(mesh):
    placed = (P(("outer", "inner"), None), P(("outer", "inner"), None), P(), P(), P())
    return jax.shard_map(
        per_device,
        mesh=mesh,
        in_specs=placed,
        out_specs=P(("outer", "inner"), None),
        check_vma=False,
    )
```

profile of v0, /device:TPU:0, one launch (start us, length us, event | category | flops | bytes accessed | tf_op | source)
XLA Modules:
  0.0 142.2 jit_solution(13806589943837288145)
XLA Ops:
  6.5 0.0 all-gather.3.cloned.1.call-start
  6.5 1.7 %multiply_reduce_fusion.1 = (f32[112]{0:T(128)S(1)}, f32[112,256]{1,0:T(8,128)}) fusion(f32[112,256]{1,0:T(8,128)} %param.5, f32[256]{0:T(256)} %param.7), kind=kLoop, calls=%fused_computation.19 | loop fusion | flops 85904 | bytes 230848 | tf_op jit(solution)/shard_map/reduce_sum | solution.py:13
  8.2 0.0 copy-start.1
  8.2 0.0 all-gather.3.cloned.1.call-update
  8.2 0.0 all-gather.5.cloned.1.call-start
  8.3 0.7 all-gather.5.cloned.1.call-update
  10.3 63.2 %all-gather.3.cloned.1.call-done = f32[3584,256]{1,0:T(8,128)} async-done(((f32[112,256]{1,0:T(8,128)}), f32[3584,256]{1,0:T(8,128)}) %all-gather.3.cloned.1.call-update) | async-done | bytes 3670032 | tf_op jit(solution)/shard_map/all_gather | solution.py:34
  73.5 0.0 copy-start
  73.5 2.7 %multiply_reduce_fusion = f32[3584]{0:T(1024)S(1)} fusion(f32[3584,256]{1,0:T(8,128)} %all-gather.3.cloned.1.call-done), kind=kLoop, calls=%fused_computation.5 | loop fusion | flops 1831424 | bytes 3684352 | tf_op jit(solution)/shard_map/reduce_sum | solution.py:13
  76.2 0.0 copy-done.1
  76.3 0.4 copy-done
  76.6 0.0 copy-start.2
  76.7 4.0 %fusion.3 = f32[112,3584]{1,0:T(8,128)S(1)} fusion(f32[112,256]{1,0:T(8,128)S(1)} %copy-done.1, f32[3584,256]{1,0:T(8,128)S(1)} %copy-done, f32[3584]{0:T(1024)S(1)} %multiply_reduce_fusion, f32[112]{0:T(128)S(1)} %get-tuple-element.5), kind=kOutput, calls=%fused_computation.4 | convolution fusion | flops 1235132416 | bytes 5405120 | tf_op jit(solution)/shard_map/dot_general | solution.py:17
  80.6 50.5 %all-gather.5.cloned.1.call-done = f32[3584,128]{1,0:T(8,128)} async-done(((f32[112,128]{1,0:T(8,128)}), f32[3584,128]{1,0:T(8,128)}) %all-gather.5.cloned.1.call-update) | async-done | bytes 1835024 | tf_op jit(solution)/shard_map/all_gather | solution.py:35
  131.2 0.0 copy-done.2
  131.2 4.2 %fusion.13 = f32[112,128]{1,0:T(8,128)} fusion(f32[3584,128]{1,0:T(8,128)} %all-gather.5.cloned.1.call-done, f32[112,3584]{1,0:T(8,128)S(1)} %fusion.3, f32[]{:T(128)} %bitcast.5, f32[112,128]{1,0:T(8,128)S(1)} %copy-done.2, f32[]{:T(128)} %bitcast.6), kind=kOutput, calls=%fused_computation.15 | convolution fusion | flops 619401216 | bytes 3555336 | tf_op jit(solution)/shard_map/dot_general | solution.py:25
Async XLA Ops:
  6.5 67.0 %all-gather.3.cloned.1.call-start = ((), (), s32[]{:S(2)}) async-start(), calls=%async_computation | async-start | bytes 3784704 | tf_op jit(solution)/shard_map/all_gather | solution.py:34
  8.2 68.0 %copy-start.1 = (f32[112,256]{1,0:T(8,128)S(1)}, f32[112,256]{1,0:T(8,128)}, u32[]{:S(2)}) copy-start(f32[112,256]{1,0:T(8,128)} %get-tuple-element.6) | copy-start | bytes 344068
  8.2 122.9 %all-gather.5.cloned.1.call-start = ((), (), s32[]{:S(2)}) async-start(), calls=%async_computation.1 | async-start | bytes 1892352 | tf_op jit(solution)/shard_map/all_gather | solution.py:35
  73.5 3.1 %copy-start = (f32[3584,256]{1,0:T(8,128)S(1)}, f32[3584,256]{1,0:T(8,128)}, u32[]{:S(2)}) copy-start(f32[3584,256]{1,0:T(8,128)} %all-gather.3.cloned.1.call-done) | copy-start | bytes 11010052
  76.6 54.5 %copy-start.2 = (f32[112,128]{1,0:T(8,128)S(1)}, f32[112,128]{1,0:T(8,128)}, u32[]{:S(2)}) copy-start(f32[112,128]{1,0:T(8,128)} %param.6) | copy-start | bytes 172036
Sparse Core Ops, SparseCore 0:
  10.2 63.2 all-gather.2
  76.4 54.7 all-gather.4
where the time goes:
time: 142 us
  waiting for transfers between devices  114 us (80%)
  between operations  14.7 us (10%)
  matrix products  8.21 us (6%)
  other arithmetic  4.39 us (3%)
    all_gather x1, waiting for transfers between devices, per_device(): piece_rows = lax.all_gather(scaled, ('outer', 'inner'), axis=0, tiled=True)  63.2 us
    all_gather x1, waiting for transfers between devices, per_device(): lax.all_gather(vectors, ('outer', 'inner'), axis=0, tiled=True)  50.5 us
    reduce_sum x2, other arithmetic, row_norms(): return jnp.sum(rows * rows, axis=1)  4.39 us
    dot_general x1, matrix products, apply_tile(): jnp.dot(tile, values, precision=lax.Precision.HIGHEST, preferred_element_...  4.23 us
    dot_general x1, matrix products, kernel_tile(): jnp.dot(rows, cols.T, precision=lax.Precision.HIGHEST, preferred_element_...  3.97 us
  transfers between devices with their start and end apart: 2, of which 2 were waited for; matrix products, arithmetic and copies ran while one was open for 5% of the time, Pallas kernels for 0%

commit v1 on v0

--- a/solution.py
+++ b/solution.py
@@ -2,6 +2,28 @@
 import jax.numpy as jnp
 from jax import lax
 from jax.sharding import PartitionSpec as P
+
+
+def laid_out(pieces, dim):
+    shape = list(pieces.shape[1:])
+    shape[dim] *= pieces.shape[0]
+    return jnp.moveaxis(pieces, 0, dim).reshape(shape)
+
+
+def doubled(x, axis):
+    size = lax.axis_size(axis)
+    pieces = x[None]
+    for level in range(size.bit_length() - 1):
+        bit = 1 << level
+        other = lax.ppermute(pieces, axis, [(i, i ^ bit) for i in range(size)])
+        both = jnp.stack([pieces, other])
+        upper = lax.axis_index(axis) >> level & 1
+        pieces = jnp.where(upper == 0, both, both[::-1]).reshape(-1, *x.shape)
+    return pieces
+
+
+def doubled_up(x, axis, dim):
+    return laid_out(doubled(x, axis), dim)
 
 
 def matern(dist2, amplitude):
@@ -32,7 +54,7 @@
     scaled = points / lengthscales[None, :]
     sqnorm = row_norms(scaled)
     piece_rows = lax.all_gather(scaled, ("outer", "inner"), axis=0, tiled=True)
-    piece_values = lax.all_gather(vectors, ("outer", "inner"), axis=0, tiled=True)
+    piece_values = doubled_up(vectors, ("outer", "inner"), 0)
     tile = kernel_tile(scaled, sqnorm, piece_rows, row_norms(piece_rows), amplitude)
     total = apply_tile(tile, piece_values)
     return total + noise[0] * vectors

time: 142 us -> 98.6 us (0.69)
  waiting for transfers between devices: 114 us -> 61.2 us
  starting transfers between devices: 0.04 us -> 8.99 us
  matrix products: 8.21 us -> 6.75 us
    all_gather x1 -> x0, waiting for transfers between devices: 50.5 us -> none  [per_device(): lax.all_gather(vectors, ('outer', 'inner'), axis=0, tiled=True)]
    all_gather x1, waiting for transfers between devices: 63.2 us -> 14.6 us  [per_device(): piece_rows = lax.all_gather(scaled, ('outer', 'inner'), axis=0, tiled=True)]
    ppermute x0 -> x5, waiting for transfers between devices: none -> 46.6 us  [doubled(): other = lax.ppermute(pieces, axis, [(i, i ^ bit) for i in range(size)])]
    ppermute x0 -> x5, starting transfers between devices: none -> 8.99 us  [doubled(): other = lax.ppermute(pieces, axis, [(i, i ^ bit) for i in range(size)])]
    dot_general x1, matrix products: 4.23 us -> 2.75 us  [apply_tile(): jnp.dot(tile, values, precision=lax.Precision.HIGHEST, preferred_element_...]
  transfers between devices with their start and end apart: 2 -> 6, of which waited for: 2 -> 6; matrix products, arithmetic and copies ran while one was open for 5% -> 1% of each run, Pallas kernels for 0% -> 0%
where the time goes in v1:
time: 98.6 us; the launch traced here: 97.9 us
  waiting for transfers between devices  61.2 us (62%)
  between operations  14.8 us (15%)
  starting transfers between devices  8.99 us (9%)
  matrix products  6.75 us (7%)
  other arithmetic  5.7 us (6%)
    ppermute x5, waiting for transfers between devices, doubled(): other = lax.ppermute(pieces, axis, [(i, i ^ bit) for i in range(size)])  46.6 us
    all_gather x1, waiting for transfers between devices, per_device(): piece_rows = lax.all_gather(scaled, ('outer', 'inner'), axis=0, tiled=True)  14.6 us
    ppermute x5, starting transfers between devices, doubled(): other = lax.ppermute(pieces, axis, [(i, i ^ bit) for i in range(size)])  8.99 us
    reduce_sum x2, other arithmetic, row_norms(): return jnp.sum(rows * rows, axis=1)  4.39 us
    dot_general x1, matrix products, kernel_tile(): jnp.dot(rows, cols.T, precision=lax.Precision.HIGHEST, preferred_element_...  4 us
    dot_general x1, matrix products, apply_tile(): jnp.dot(tile, values, precision=lax.Precision.HIGHEST, preferred_element_...  2.75 us
  transfers between devices with their start and end apart: 6, of which 6 were waited for; matrix products, arithmetic and copies ran while one was open for 1% of the time, Pallas kernels for 0%

profile of v1, /device:TPU:0, one launch (start us, length us, event | category | flops | bytes accessed | tf_op | source)
XLA Modules:
  0.0 97.9 jit_solution(18083104482992495631)
XLA Ops:
  6.5 0.0 all-gather.2.cloned.1.call-start
  6.5 1.7 %multiply_reduce_fusion.1 = (f32[112]{0:T(128)S(1)}, f32[112,256]{1,0:T(8,128)}) fusion(f32[112,256]{1,0:T(8,128)} %param.5, f32[256]{0:T(256)} %param.7), kind=kLoop, calls=%fused_computation.29 | loop fusion | flops 85904 | bytes 230848 | tf_op jit(solution)/shard_map/reduce_sum | solution.py:35
  8.2 0.0 all-gather.2.cloned.1.call-update
  8.2 0.5 collective-permute-start
  8.7 1.1 %collective-permute-done = f32[1,112,128]{2,1,0:T(8,128)S(1)} collective-permute-done((f32[1,112,128]{2,1,0:T(8,128)}, f32[1,112,128]{2,1,0:T(8,128)S(1)}, u32[]{:S(2)}, u32[]{:S(2)}) %collective-permute-start) | collective-permute-done | bytes 57376 | tf_op jit(solution)/shard_map/ppermute | solution.py:18
  9.8 0.8 pad_maximum_fusion.4
  10.7 3.0 %collective-permute-start.1 = (f32[2,112,128]{2,1,0:T(8,128)S(1)}, f32[2,112,128]{2,1,0:T(8,128)S(1)}, u32[]{:S(2)}, u32[]{:S(2)}) collective-permute-start(f32[2,112,128]{2,1,0:T(8,128)S(1)} %get-tuple-element.8), channel_id=1, source_target_pairs={{0,2},{1,3},{2,0},{3,1},{4,6},{5,7},{6,4},{7,5},{8,10},{9,11},{10,... | collective-permute-start | bytes 344072 | tf_op jit(solution)/shard_map/ppermute | solution.py:18
  13.7 3.5 %collective-permute-done.1 = f32[2,112,128]{2,1,0:T(8,128)S(1)} collective-permute-done((f32[2,112,128]{2,1,0:T(8,128)S(1)}, f32[2,112,128]{2,1,0:T(8,128)S(1)}, u32[]{:S(2)}, u32[]{:S(2)}) %collective-permute-start.1) | collective-permute-done | bytes 114720 | tf_op jit(solution)/shard_map/ppermute | solution.py:18
  17.2 2.8 %collective-permute-start.2 = (f32[4,112,128]{2,1,0:T(8,128)S(1)}, f32[4,112,128]{2,1,0:T(8,128)S(1)}, u32[]{:S(2)}, u32[]{:S(2)}) collective-permute-start(f32[4,112,128]{2,1,0:T(8,128)S(1)} %bitcast.31), channel_id=1, source_target_pairs={{0,4},{1,5},{2,6},{3,7},{4,0},{5,1},{6,2},{7,3},{8,12},{9,13},{10,... | collective-permute-start | bytes 688136 | tf_op jit(solution)/shard_map/ppermute | solution.py:18
  20.0 12.0 %collective-permute-done.2 = f32[4,112,128]{2,1,0:T(8,128)S(1)} collective-permute-done((f32[4,112,128]{2,1,0:T(8,128)S(1)}, f32[4,112,128]{2,1,0:T(8,128)S(1)}, u32[]{:S(2)}, u32[]{:S(2)}) %collective-permute-start.2) | collective-permute-done | bytes 229408 | tf_op jit(solution)/shard_map/ppermute | solution.py:18
  32.1 1.4 %collective-permute-start.3 = (f32[8,112,128]{2,1,0:T(8,128)S(1)}, f32[8,112,128]{2,1,0:T(8,128)S(1)}, u32[]{:S(2)}, u32[]{:S(2)}) collective-permute-start(f32[8,112,128]{2,1,0:T(8,128)S(1)} %bitcast.28), channel_id=1, source_target_pairs={{0,8},{1,9},{2,10},{3,11},{4,12},{5,13},{6,14},{7,15},{8,0},{9,1},... | collective-permute-start | bytes 1376264 | tf_op jit(solution)/shard_map/ppermute | solution.py:18
  33.4 11.9 %collective-permute-done.3 = f32[8,112,128]{2,1,0:T(8,128)S(1)} collective-permute-done((f32[8,112,128]{2,1,0:T(8,128)S(1)}, f32[8,112,128]{2,1,0:T(8,128)S(1)}, u32[]{:S(2)}, u32[]{:S(2)}) %collective-permute-start.3) | collective-permute-done | bytes 458784 | tf_op jit(solution)/shard_map/ppermute | solution.py:18
  45.3 0.1 pad_maximum_fusion.1
  45.3 0.1 reverse_select_fusion.1
  45.4 1.3 %collective-permute-start.4 = (f32[16,112,128]{2,1,0:T(8,128)S(1)}, f32[16,112,128]{2,1,0:T(8,128)S(1)}, u32[]{:S(2)}, u32[]{:S(2)}) collective-permute-start(f32[16,112,128]{2,1,0:T(8,128)S(1)} %bitcast.26), channel_id=1, source_target_pairs={{0,16},{1,17},{2,18},{3,19},{4,20},{5,21},{6,22},{7,23},{8,24},{9,... | collective-permute-start | bytes 2752520 | tf_op jit(solution)/shard_map/ppermute | solution.py:18
  48.0 18.3 %collective-permute-done.4 = f32[16,112,128]{2,1,0:T(8,128)S(1)} collective-permute-done((f32[16,112,128]{2,1,0:T(8,128)S(1)}, f32[16,112,128]{2,1,0:T(8,128)S(1)}, u32[]{:S(2)}, u32[]{:S(2)}) %collective-permute-start.4) | collective-permute-done | bytes 917536 | tf_op jit(solution)/shard_map/ppermute | solution.py:18
  66.3 0.1 pad_maximum_fusion
  66.4 0.0 copy-start.1
  66.4 0.1 reverse_select_fusion
  66.5 14.6 %all-gather.2.cloned.1.call-done = f32[3584,256]{1,0:T(8,128)} async-done(((f32[112,256]{1,0:T(8,128)}), f32[3584,256]{1,0:T(8,128)}) %all-gather.2.cloned.1.call-update) | async-done | bytes 3670032 | tf_op jit(solution)/shard_map/all_gather | solution.py:56
  81.1 0.0 copy-start
  81.1 2.7 %multiply_reduce_fusion = f32[3584]{0:T(1024)S(1)} fusion(f32[3584,256]{1,0:T(8,128)} %all-gather.2.cloned.1.call-done), kind=kLoop, calls=%fused_computation.5 | loop fusion | flops 1831424 | bytes 3684352 | tf_op jit(solution)/shard_map/reduce_sum | solution.py:35
  83.9 0.0 copy-done.1
  83.9 0.4 copy-done
  84.3 0.0 copy-start.2
  84.3 4.0 %fusion.3 = f32[112,3584]{1,0:T(8,128)S(1)} fusion(f32[112,256]{1,0:T(8,128)S(1)} %copy-done.1, f32[3584,256]{1,0:T(8,128)S(1)} %copy-done, f32[3584]{0:T(1024)S(1)} %multiply_reduce_fusion, f32[112]{0:T(128)S(1)} %get-tuple-element.5), kind=kOutput, calls=%fused_computation.4 | convolution fusion | flops 1235132416 | bytes 5405120 | tf_op jit(solution)/shard_map/dot_general | solution.py:39
  88.3 0.0 copy-done.2
  88.3 2.7 %fusion.13 = f32[112,128]{1,0:T(8,128)} fusion(f32[3584,128]{1,0:T(8,128)S(1)} %bitcast.25, f32[112,3584]{1,0:T(8,128)S(1)} %fusion.3, f32[]{:T(128)} %bitcast.23, f32[112,128]{1,0:T(8,128)S(1)} %copy-done.2, f32[]{:T(128)} %bitcast.24), kind=kOutput, calls=%fused_computation.18 | convolution fusion | flops 619401216 | bytes 3555336 | tf_op jit(solution)/shard_map/dot_general | solution.py:47
  (5 shorter events, 0.1 us)
Async XLA Ops:
  6.5 74.6 %all-gather.2.cloned.1.call-start = ((), (), s32[]{:S(2)}) async-start(), calls=%async_computation | async-start | bytes 3784704 | tf_op jit(solution)/shard_map/all_gather | solution.py:56
  8.2 1.6 %collective-permute-start = (f32[1,112,128]{2,1,0:T(8,128)}, f32[1,112,128]{2,1,0:T(8,128)S(1)}, u32[]{:S(2)}, u32[]{:S(2)}) collective-permute-start(f32[1,112,128]{2,1,0:T(8,128)} %bitcast.35), channel_id=1, source_target_pairs={{0,1},{1,0},{2,3},{3,2},{4,5},{5,4},{6,7},{7,6},{8,9},{9,8},{10,11... | collective-permute-start | bytes 172040 | tf_op jit(solution)/shard_map/ppermute | solution.py:18
  10.7 6.5 %collective-permute-start.1 = (f32[2,112,128]{2,1,0:T(8,128)S(1)}, f32[2,112,128]{2,1,0:T(8,128)S(1)}, u32[]{:S(2)}, u32[]{:S(2)}) collective-permute-start(f32[2,112,128]{2,1,0:T(8,128)S(1)} %get-tuple-element.8), channel_id=1, source_target_pairs={{0,2},{1,3},{2,0},{3,1},{4,6},{5,7},{6,4},{7,5},{8,10},{9,11},{10,... | collective-permute-start | bytes 344072 | tf_op jit(solution)/shard_map/ppermute | solution.py:18
  17.2 14.8 %collective-permute-start.2 = (f32[4,112,128]{2,1,0:T(8,128)S(1)}, f32[4,112,128]{2,1,0:T(8,128)S(1)}, u32[]{:S(2)}, u32[]{:S(2)}) collective-permute-start(f32[4,112,128]{2,1,0:T(8,128)S(1)} %bitcast.31), channel_id=1, source_target_pairs={{0,4},{1,5},{2,6},{3,7},{4,0},{5,1},{6,2},{7,3},{8,12},{9,13},{10,... | collective-permute-start | bytes 688136 | tf_op jit(solution)/shard_map/ppermute | solution.py:18
  32.1 13.2 %collective-permute-start.3 = (f32[8,112,128]{2,1,0:T(8,128)S(1)}, f32[8,112,128]{2,1,0:T(8,128)S(1)}, u32[]{:S(2)}, u32[]{:S(2)}) collective-permute-start(f32[8,112,128]{2,1,0:T(8,128)S(1)} %bitcast.28), channel_id=1, source_target_pairs={{0,8},{1,9},{2,10},{3,11},{4,12},{5,13},{6,14},{7,15},{8,0},{9,1},... | collective-permute-start | bytes 1376264 | tf_op jit(solution)/shard_map/ppermute | solution.py:18
  45.4 20.9 %collective-permute-start.4 = (f32[16,112,128]{2,1,0:T(8,128)S(1)}, f32[16,112,128]{2,1,0:T(8,128)S(1)}, u32[]{:S(2)}, u32[]{:S(2)}) collective-permute-start(f32[16,112,128]{2,1,0:T(8,128)S(1)} %bitcast.26), channel_id=1, source_target_pairs={{0,16},{1,17},{2,18},{3,19},{4,20},{5,21},{6,22},{7,23},{8,24},{9,... | collective-permute-start | bytes 2752520 | tf_op jit(solution)/shard_map/ppermute | solution.py:18
  66.4 17.5 %copy-start.1 = (f32[112,256]{1,0:T(8,128)S(1)}, f32[112,256]{1,0:T(8,128)}, u32[]{:S(2)}) copy-start(f32[112,256]{1,0:T(8,128)} %get-tuple-element.6) | copy-start | bytes 344068
  81.1 3.1 %copy-start = (f32[3584,256]{1,0:T(8,128)S(1)}, f32[3584,256]{1,0:T(8,128)}, u32[]{:S(2)}) copy-start(f32[3584,256]{1,0:T(8,128)} %all-gather.2.cloned.1.call-done) | copy-start | bytes 11010052
  84.3 4.0 %copy-start.2 = (f32[112,128]{1,0:T(8,128)S(1)}, f32[112,128]{1,0:T(8,128)}, u32[]{:S(2)}) copy-start(f32[112,128]{1,0:T(8,128)} %param.6) | copy-start | bytes 172036
Sparse Core Ops, SparseCore 0:
  10.2 70.8 all-gather.1
